TPU v7x, 32 devices: a whole 2x2x4 slice. The times are simulated.
32 devices in a mesh: groups: 2 (over x), gx: 16 (over z, y, core).
Axes of the slice: x: 2, y: 2, z: 4, core: 2. Of those that a mesh axis runs over, the one named last changes fastest.
Arguments:
- checkpoint: float32 [19, 64, 128, 128], P(None, 'gx', 'groups'), parts along dimension 2, as said below
- adjoint_seed: float32 [19, 64, 128, 128], P(None, 'gx', 'groups'), parts along dimension 2, may hold values from -6 to 6
- material: int32 [64, 128, 128], P('gx', 'groups'), parts along dimension 1, may hold values from 0 to 7
- wall_mask: int32 [64, 128, 128], P('gx', 'groups'), parts along dimension 1, may hold values from 0 to 1, as said below
- class_porosity: float32 [8], replicated, may hold values from 0.3 to 1
- step_index: int32 [2], P('groups'), parts along dimension 0, may hold values from 0 to 999
Outputs:
- adjoint_states: float32 [19, 64, 128, 128], P(None, 'gx', 'groups'), parts along dimension 2
- porosity_grad: float32 [64, 128, 128], P('gx', 'groups'), parts along dimension 1
There are 2 independent parts, one for each index of `groups`. A program takes and returns all parts, laid end to end along the dimension named above; an argument that names none is the same for every part. Nothing has to cross between parts.
Inputs may be any that keep to these rules, and one draw needn't show every extreme that they name: `wall_mask`: cells at z = 0 and z = 127 are walls. `checkpoint`: populations are positive, with density near 1.
All inputs are finite; a program needn't handle non-finite values.
Results may differ from a plain program's by a relative error of at most 0.0003.
Values sent between devices are 32-bit elements; how exact they have to be, the bound alone decides.
A program may use at most 64 MiB of HBM per device.

v0:
```python
import functools

import jax
import jax.numpy as jnp
import numpy as np
from jax import lax
from jax.experimental import pallas as pl
from jax.experimental.pallas import tpu as pltpu
from jax.sharding import PartitionSpec as P

MESH = pl.DeviceIdType.MESH
ROWS = 8


def velocity_list():
    rows = [(0, 0, 0)]
    for axis in range(3):
        for sign in (1, -1):
            entry = [0, 0, 0]
            entry[axis] = sign
            rows.append(tuple(entry))
    for first, second in ((0, 1), (0, 2), (1, 2)):
        for one in (1, -1):
            for two in (1, -1):
                entry = [0, 0, 0]
                entry[first] = one
                entry[second] = two
                rows.append(tuple(entry))
    return rows


VEL = velocity_list()
PLUS = [q for q in range(19) if VEL[q][0] == 1]
MINUS = [q for q in range(19) if VEL[q][0] == -1]
REST = [q for q in range(19) if VEL[q][0] == 0]
SLOT = {q: pos for pos, q in enumerate(PLUS + MINUS + REST)}
SAME = {q: q for q in range(19)}
AXIS = [(VEL.index(tuple(int(a == d) for d in range(3))),
         VEL.index(tuple(-int(a == d) for d in range(3)))) for a in range(3)]
PLANES = ((0, 1), (0, 2), (1, 2))


def corner(plane, one, two):
    entry = [0, 0, 0]
    entry[plane[0]] = one
    entry[plane[1]] = two
    return VEL.index(tuple(entry))


def to_pairs(f):
    sums = [f[p] + f[m] for p, m in AXIS]
    diffs = [f[p] - f[m] for p, m in AXIS]
    quads = []
    for plane in PLANES:
        pp, pm = f[corner(plane, 1, 1)], f[corner(plane, 1, -1)]
        mp, mm = f[corner(plane, -1, 1)], f[corner(plane, -1, -1)]
        s1, d1, s2, d2 = pp + pm, pp - pm, mp + mm, mp - mm
        quads.append((s1 + s2, d1 - d2, s1 - s2, d1 + d2))
    return f[0], sums, diffs, quads


def from_pairs(rest, sums, diffs, quads):
    out = {0: rest}
    for a, (p, m) in enumerate(AXIS):
        out[p] = sums[a] + diffs[a]
        out[m] = sums[a] - diffs[a]
    for plane, (qa, qb, qc, qd) in zip(PLANES, quads):
        s1, s2, d1, d2 = qa + qc, qa - qc, qb + qd, qd - qb
        out[corner(plane, 1, 1)] = s1 + d1
        out[corner(plane, 1, -1)] = s1 - d1
        out[corner(plane, -1, 1)] = s2 + d2
        out[corner(plane, -1, -1)] = s2 - d2
    return out


def conserved(rest, sums, diffs, quads):
    axy, axz, ayz = quads[0][0], quads[1][0], quads[2][0]
    density = (rest + (sums[0] + sums[1])) + (sums[2] + axy) + (axz + ayz)
    jx = diffs[0] + (quads[0][2] + quads[1][2])
    jy = diffs[1] + (quads[0][3] + quads[2][2])
    jz = diffs[2] + (quads[1][3] + quads[2][3])
    return density, (jx, jy, jz)


def rates(wall):
    pick = lambda at_wall, inside: jnp.where(wall, jnp.float32(at_wall), jnp.float32(inside))
    return dict(k2=pick(1, -0.6), s2=pick(0, 1.6), k3=pick(-1, -0.4), s3=pick(0, 1.4 / 3.0),
                k4=pick(1, -0.2), s4=pick(0, 1.2), sg=pick(-1, 1))


def forward(f, porosity, wall, force):
    k = rates(wall)
    rest, sums, diffs, quads = to_pairs(f)
    density, j = conserved(rest, sums, diffs, quads)
    ratio = porosity / density
    q = [porosity * c for c in j]
    u = [ratio * c for c in j]
    pxx, pyy, pzz = [q[a] * u[a] for a in range(3)]
    push = jnp.where(wall, 0.0, force)
    push3 = push * (1.0 / 3.0)
    third = density * (1.0 / 3.0)
    ninth = density * (1.0 / 9.0)
    a_of = [quads[n][0] for n in range(3)]
    even = [ninth + (pxx + pyy) * (1.0 / 3.0) - pzz * (1.0 / 6.0),
            ninth + (pxx + pzz) * (1.0 / 3.0) - pyy * (1.0 / 6.0),
            ninth + (pyy + pzz) * (1.0 / 3.0) - pxx * (1.0 / 6.0)]
    m = [sums[0] + (a_of[0] + a_of[1]), sums[1] + (a_of[0] + a_of[2]), sums[2] + (a_of[1] + a_of[2])]
    ms = [k["k2"] * m[a] + k["s2"] * (third + p) for a, p in enumerate((pxx, pyy, pzz))]
    new = []
    odd = [k["s3"] * q[0] + push3, k["s3"] * q[1], k["s3"] * q[2]]
    for n, (a, b) in enumerate(PLANES):
        qa, qb, qc, qd = quads[n]
        new.append((k["k4"] * qa + k["s4"] * even[n],
                    k["k2"] * qb + k["s2"] * (q[a] * u[b]),
                    k["k3"] * qc + odd[a],
                    k["k3"] * qd + odd[b]))
    axy, axz, ayz = new[0][0], new[1][0], new[2][0]
    s_new = [ms[0] - (axy + axz), ms[1] - (axy + ayz), ms[2] - (axz + ayz)]
    d_new = [(k["sg"] * j[0] + push) - (new[0][2] + new[1][2]),
             k["sg"] * j[1] - (new[0][3] + new[2][2]),
             k["sg"] * j[2] - (new[1][3] + new[2][3])]
    rest_new = density - (ms[0] + ms[1] + ms[2]) + (axy + axz + ayz)
    out = from_pairs(rest_new, [0.5 * s for s in s_new], [0.5 * d for d in d_new],
                     [tuple(0.25 * v for v in quad) for quad in new])
    return out, j, ratio


def backward(h, j, ratio, porosity, wall):
    k = rates(wall)
    h0, hs, hd, hq = to_pairs(h)
    hs = [0.5 * v for v in hs]
    hd = [0.5 * v for v in hd]
    hq = [tuple(0.25 * v for v in quad) for quad in hq]
    u = [ratio * c for c in j]
    ts = [v - h0 for v in hs]
    ta = [hq[n][0] - h0 - (ts[a] + ts[b]) for n, (a, b) in enumerate(PLANES)]
    tc = [(hq[n][2] - hd[a], hq[n][3] - hd[b]) for n, (a, b) in enumerate(PLANES)]
    ea = [k["s4"] * v for v in ta]
    eb = [k["s2"] * quad[1] for quad in hq]
    em = [k["s2"] * v for v in ts]
    px = em[0] + (ea[0] + ea[1]) * (1.0 / 3.0) - ea[2] * (1.0 / 6.0)
    py = em[1] + (ea[0] + ea[2]) * (1.0 / 3.0) - ea[1] * (1.0 / 6.0)
    pz = em[2] + (ea[1] + ea[2]) * (1.0 / 3.0) - ea[0] * (1.0 / 6.0)
    gx = 2.0 * px * u[0] + (eb[0] * u[1] + eb[1] * u[2])
    gy = 2.0 * py * u[1] + (eb[0] * u[0] + eb[2] * u[2])
    gz = 2.0 * pz * u[2] + (eb[1] * u[0] + eb[2] * u[1])
    a_rho = (h0 + (em[0] + em[1] + em[2]) * (1.0 / 3.0) + (ea[0] + ea[1] + ea[2]) * (1.0 / 9.0)
             - 0.5 * (u[0] * gx + u[1] * gy + u[2] * gz))
    g = [gx + k["s3"] * (tc[0][0] + tc[1][0]),
         gy + k["s3"] * (tc[0][1] + tc[2][0]),
         gz + k["s3"] * (tc[1][1] + tc[2][1])]
    grad = j[0] * g[0] + j[1] * g[1] + j[2] * g[2]
    aj = [k["sg"] * hd[a] + porosity * g[a] for a in range(3)]
    am = [k["k2"] * v for v in ts]
    quads = []
    for n, (a, b) in enumerate(PLANES):
        quads.append((k["k4"] * ta[n] + a_rho + (am[a] + am[b]),
                      k["k2"] * hq[n][1],
                      k["k3"] * tc[n][0] + aj[a],
                      k["k3"] * tc[n][1] + aj[b]))
    out = from_pairs(a_rho, [a_rho + v for v in am], aj, quads)
    return out, grad


def kernel(axis, poro_ref, step_ref, chk_hbm, seed_hbm, mat_hbm, wall_hbm, out_hbm, grad_hbm,
           chk, mat, wal, seed, post, adj, mom, por, out, grad,
           load_sem, send_sem, recv_sem, out_sem):
    width, ny, nz = mat.shape
    steps = ny // ROWS
    count = lax.axis_size(axis)
    me = lax.axis_index(axis)
    right, left = lax.rem(me + 1, count), lax.rem(me + count - 1, count)
    last = width - 1
    edge = [0, last] if width > 1 else [0]
    inner = max(width - 2, 0)

    barrier = pltpu.get_barrier_semaphore()
    for neighbour in (left, right):
        pl.semaphore_signal(barrier, inc=1, device_id={axis: neighbour}, device_id_type=MESH)

    loads = [pltpu.make_async_copy(mat_hbm, mat, load_sem.at[0]),
             pltpu.make_async_copy(wall_hbm, wal, load_sem.at[1])]
    edge_loads = [pltpu.make_async_copy(chk_hbm.at[:, x], chk.at[:, x], load_sem.at[2 + n])
                  for n, x in enumerate(edge)]
    late = []
    if inner:
        late.append(pltpu.make_async_copy(chk_hbm.at[:, pl.ds(1, inner)], chk.at[:, pl.ds(1, inner)],
                                          load_sem.at[4]))
    seed_load = pltpu.make_async_copy(seed_hbm, seed.at[:, pl.ds(1, width)], load_sem.at[5])
    for copy in loads + edge_loads + late + [seed_load]:
        copy.start()

    def remote(src, dst, number, target):
        return pltpu.make_async_remote_copy(
            src_ref=src, dst_ref=dst, send_sem=send_sem.at[number], recv_sem=recv_sem.at[number],
            device_id={axis: target}, device_id_type=MESH)

    seed_sends = []
    for start, size in ((1, 1), (7, 2), (11, 2)):
        seed_sends.append(remote(seed_hbm.at[pl.ds(start, size), 0],
                                 seed.at[pl.ds(start, size), width + 1], len(seed_sends), left))
    for start, size in ((2, 1), (9, 2), (13, 2)):
        seed_sends.append(remote(seed_hbm.at[pl.ds(start, size), last],
                                 seed.at[pl.ds(start, size), 0], len(seed_sends), right))
    post_up = remote(post.at[pl.ds(0, 5), width], post.at[pl.ds(0, 5), 0], 6, right)
    post_down = remote(post.at[pl.ds(5, 5), 1], post.at[pl.ds(5, 5), width + 1], 7, left)
    adj_down = remote(adj.at[pl.ds(0, 5), 1], adj.at[pl.ds(0, 5), width + 1], 8, left)
    adj_up = remote(adj.at[pl.ds(5, 5), width], adj.at[pl.ds(5, 5), 0], 9, right)

    row = lax.broadcasted_iota(jnp.int32, (ROWS, nz), 0)
    turn = (step_ref[0] & 63).astype(jnp.float32) * np.float32(2.0 * np.pi / 64.0)
    force = 0.05 * jnp.sin(jnp.full((ROWS, nz), turn, jnp.float32))

    def shifted(ref, slot, layer, i, sy, sz):
        value = ref[slot, layer, pl.ds(pl.multiple_of(i * ROWS, ROWS), ROWS), :]
        if sy:
            near = lax.rem(i + (steps - 1 if sy > 0 else 1), steps)
            other = ref[slot, layer, pl.ds(pl.multiple_of(near * ROWS, ROWS), ROWS), :]
            value = jnp.where(row == (ROWS - 1 if sy > 0 else 0), other, value)
            value = pltpu.roll(value, sy % ROWS, 0)
        if sz:
            value = pltpu.roll(value, sz % nz, 1)
        return value

    def streamed(ref, x, i, sign, slots):
        return [shifted(ref, slots[q], x + 1 - sign * VEL[q][0], i, sign * VEL[q][1],
                        sign * VEL[q][2]) for q in range(19)]

    def over(layers, body):
        first, stride, number = layers
        if number == 0:
            return

        def step(t, carry):
            body(first + stride * (t // steps), lax.rem(t, steps))
            return carry

        lax.fori_loop(0, number * steps, step, 0)

    edges = (0, max(last, 1), len(edge))
    middle = (1, 1, inner)

    def here(i):
        return pl.ds(pl.multiple_of(i * ROWS, ROWS), ROWS)

    def collide(x, i):
        at = here(i)
        kinds = mat[x, at, :]
        porosity = jnp.zeros((ROWS, nz), jnp.float32)
        for number in range(poro_ref.shape[0]):
            porosity = jnp.where(kinds == number, poro_ref[number], porosity)
        f = [chk[q, x, at, :] for q in range(19)]
        g, j, ratio = forward(f, porosity, wal[x, at, :] == 1, force)
        for q in range(19):
            post[SLOT[q], x + 1, at, :] = g[q]
        por[x, at, :] = porosity
        for n, value in enumerate((*j, ratio)):
            mom[n, x, at, :] = value

    def back_one(x, i):
        at = here(i)
        porosity = por[x, at, :]
        density, j = conserved(*to_pairs(streamed(post, x, i, 1, SLOT)))
        h = streamed(seed, x, i, -1, SAME)
        a, part = backward(h, j, porosity / density, porosity, wal[x, at, :] == 1)
        for q in range(19):
            adj[SLOT[q], x + 1, at, :] = a[q]
        grad[x, at, :] = part

    def back_zero(x, i):
        at = here(i)
        h = streamed(adj, x, i, -1, SLOT)
        j = [mom[n, x, at, :] for n in range(3)]
        a, part = backward(h, j, mom[3, x, at, :], por[x, at, :], wal[x, at, :] == 1)
        for q in range(19):
            out[q, x, at, :] = a[q]
        grad[x, at, :] = grad[x, at, :] + part

    pl.semaphore_wait(barrier, 2)
    for copy in seed_sends:
        copy.start()
    for copy in loads + edge_loads:
        copy.wait()
    over(edges, collide)
    post_up.start()
    post_down.start()
    for copy in late:
        copy.wait()
    over(middle, collide)
    seed_load.wait()
    over(middle, back_one)
    for copy in seed_sends + [post_up, post_down]:
        copy.wait_recv()
    over(edges, back_one)
    adj_up.start()
    adj_down.start()
    over(middle, back_zero)
    stores = []
    if inner:
        stores.append(pltpu.make_async_copy(out.at[:, pl.ds(1, inner)], out_hbm.at[:, pl.ds(1, inner)],
                                            out_sem.at[0]))
        stores[-1].start()
    adj_up.wait_recv()
    adj_down.wait_recv()
    over(edges, back_zero)
    for n, x in enumerate(edge):
        stores.append(pltpu.make_async_copy(out.at[:, x], out_hbm.at[:, x], out_sem.at[1 + n]))
    stores.append(pltpu.make_async_copy(grad, grad_hbm, out_sem.at[3]))
    for copy in stores[-1 - len(edge):]:
        copy.start()
    for copy in seed_sends + [post_up, post_down, adj_up, adj_down]:
        copy.wait_send()
    for copy in stores:
        copy.wait()


def local(checkpoint, adjoint_seed, material, wall_mask, class_porosity, step_index):
    width, ny, nz = material.shape
    f32 = jnp.float32
    anywhere = pl.BlockSpec(memory_space=pl.ANY)
    scalars = pl.BlockSpec(memory_space=pltpu.SMEM)
    return pl.pallas_call(
        functools.partial(kernel, "gx"),
        out_shape=(jax.ShapeDtypeStruct(checkpoint.shape, f32),
                   jax.ShapeDtypeStruct(material.shape, f32)),
        in_specs=[scalars, scalars] + [anywhere] * 4,
        out_specs=(anywhere, anywhere),
        scratch_shapes=[
            pltpu.VMEM((19, width, ny, nz), f32),
            pltpu.VMEM((width, ny, nz), jnp.int32),
            pltpu.VMEM((width, ny, nz), jnp.int32),
            pltpu.VMEM((19, width + 2, ny, nz), f32),
            pltpu.VMEM((19, width + 2, ny, nz), f32),
            pltpu.VMEM((19, width + 2, ny, nz), f32),
            pltpu.VMEM((4, width, ny, nz), f32),
            pltpu.VMEM((width, ny, nz), f32),
            pltpu.VMEM((19, width, ny, nz), f32),
            pltpu.VMEM((width, ny, nz), f32),
            pltpu.SemaphoreType.DMA((6,)),
            pltpu.SemaphoreType.DMA((10,)),
            pltpu.SemaphoreType.DMA((10,)),
            pltpu.SemaphoreType.DMA((4,)),
        ],
        compiler_params=pltpu.CompilerParams(
            collective_id=0, has_side_effects=True, vmem_limit_bytes=44 * 2**20),
    )(class_porosity, step_index, checkpoint, adjoint_seed, material, wall_mask)


def solution(mesh):
    placed = (
        P(None, "gx", "groups", None),
        P(None, "gx", "groups", None),
        P("gx", "groups", None),
        P("gx", "groups", None),
        P(),
        P("groups"),
    )
    return jax.shard_map(
        local,
        mesh=mesh,
        in_specs=placed,
        out_specs=(P(None, "gx", "groups", None), P("gx", "groups", None)),
        check_vma=False,
    )
```

profile of v0, /device:TPU:0, one launch (start us, length us, event | category | flops | bytes accessed | tf_op | source)
XLA Modules:
  0.0 32.1 jit_solution(1335258194828919732)
XLA Ops:
  1.3 0.0 copy-start
  1.3 1.7 %copy-done = f32[19,4,64,128]{3,2,1,0:T(8,128)S(1)} copy-done((f32[19,4,64,128]{3,2,1,0:T(8,128)S(1)}, f32[19,4,64,128]{3,2,1,0:T(8,128)}, u32[]{:S(2)}) %copy-start) | copy-done | bytes 2490392
  3.0 0.0 copy-start.1
  3.0 1.7 %copy-done.1 = f32[19,4,64,128]{3,2,1,0:T(8,128)S(1)} copy-done((f32[19,4,64,128]{3,2,1,0:T(8,128)S(1)}, f32[19,4,64,128]{3,2,1,0:T(8,128)}, u32[]{:S(2)}) %copy-start.1) | copy-done | bytes 2490392
  4.7 0.0 copy-start.2
  4.7 0.9 %copy-done.2 = s32[4,64,128]{2,1,0:T(8,128)S(1)} copy-done((s32[4,64,128]{2,1,0:T(8,128)S(1)}, s32[4,64,128]{2,1,0:T(8,128)}, u32[]{:S(2)}) %copy-start.2) | copy-done | bytes 131096
  5.6 0.0 copy-start.3
  5.6 0.9 %copy-done.3 = s32[4,64,128]{2,1,0:T(8,128)S(1)} copy-done((s32[4,64,128]{2,1,0:T(8,128)S(1)}, s32[4,64,128]{2,1,0:T(8,128)}, u32[]{:S(2)}) %copy-start.3) | copy-done | bytes 131096
  6.5 0.0 copy-start.4
  6.5 0.7 %copy-done.4 = f32[8]{0:T(128)S(1)} copy-done((f32[8]{0:T(128)S(1)}, f32[8]{0:T(128)}, u32[]{:S(2)}) %copy-start.4) | copy-done | bytes 56
  7.2 22.8 %shard_map.77 = (f32[19,4,64,128]{3,2,1,0:T(8,128)S(1)}, f32[4,64,128]{2,1,0:T(8,128)S(1)}) custom-call(f32[8]{0:T(128)S(1)} %copy-done.4, s32[1]{0:T(128)S(6)} %copy.10.step_ref, f32[19,4,64,128]{3,2,1,0:T(8,128)S(1)} %copy-done, f32[19,4,64,128]{3,2,1,0:T(8,128)S(1)} %copy-done.1, s32[4,64,128]{2,1,0:T(8,128)S(1)} %copy-done.2, s32[4,64,128]{2,1,0:T(8,128)S(1)} %copy-done.3), custom_call_target="tpu_custom_call" | custom-call | tf_op jit(solution)/shard_map/pallas_call | solution.py:322
  30.0 1.5 %copy.11 = f32[19,4,64,128]{3,2,1,0:T(8,128)} copy(f32[19,4,64,128]{3,2,1,0:T(8,128)S(1)} %get-tuple-element.4) | data formatting | bytes 4980736
  31.4 0.7 %copy.12 = f32[4,64,128]{2,1,0:T(8,128)} copy(f32[4,64,128]{2,1,0:T(8,128)S(1)} %get-tuple-element.5) | data formatting | bytes 262144
Async XLA Ops:
  1.3 1.7 %copy-start = (f32[19,4,64,128]{3,2,1,0:T(8,128)S(1)}, f32[19,4,64,128]{3,2,1,0:T(8,128)}, u32[]{:S(2)}) copy-start(f32[19,4,64,128]{3,2,1,0:T(8,128)} %chk_hbm.1) | copy-start | bytes 7471108
  3.0 1.7 %copy-start.1 = (f32[19,4,64,128]{3,2,1,0:T(8,128)S(1)}, f32[19,4,64,128]{3,2,1,0:T(8,128)}, u32[]{:S(2)}) copy-start(f32[19,4,64,128]{3,2,1,0:T(8,128)} %seed_hbm.1) | copy-start | bytes 7471108
  4.7 0.9 %copy-start.2 = (s32[4,64,128]{2,1,0:T(8,128)S(1)}, s32[4,64,128]{2,1,0:T(8,128)}, u32[]{:S(2)}) copy-start(s32[4,64,128]{2,1,0:T(8,128)} %mat_hbm.1) | copy-start | bytes 393220
  5.6 0.9 %copy-start.3 = (s32[4,64,128]{2,1,0:T(8,128)S(1)}, s32[4,64,128]{2,1,0:T(8,128)}, u32[]{:S(2)}) copy-start(s32[4,64,128]{2,1,0:T(8,128)} %wall_hbm.1) | copy-start | bytes 393220
  6.5 0.7 %copy-start.4 = (f32[8]{0:T(128)S(1)}, f32[8]{0:T(128)}, u32[]{:S(2)}) copy-start(f32[8]{0:T(128)} %poro_ref.1) | copy-start | bytes 100
where the time goes:
time: 32.3 us; the launch traced here: 32.1 us
  Pallas kernels  22.8 us (71%)
  local copies, waits for them, and re-layouts  7.97 us (25%)
  between operations  1.3 us (4%)
    pallas_call x1, Pallas kernels, local(): pl.pallas_call(functools.partial(kernel, 'gx'), out_shape=(jax.ShapeDtype...  22.8 us
    unnamed x12, local copies, waits for them, and re-layouts  7.97 us

commit v1 on v0

--- a/solution.py
+++ b/solution.py
@@ -10,6 +10,7 @@
 
 MESH = pl.DeviceIdType.MESH
 ROWS = 8
+UNROLL = 4
 
 
 def velocity_list():
@@ -162,8 +163,8 @@
     return out, grad
 
 
-def kernel(axis, poro_ref, step_ref, chk_hbm, seed_hbm, mat_hbm, wall_hbm, out_hbm, grad_hbm,
-           chk, mat, wal, seed, post, adj, mom, por, out, grad,
+def kernel(axis, poro_hbm, step_ref, chk_hbm, seed_hbm, mat_hbm, wall_hbm, out_hbm, grad_hbm,
+           poro_ref, chk, mat, wal, seed, post, adj, mom, por, out, grad, face, halo,
            load_sem, send_sem, recv_sem, out_sem):
     width, ny, nz = mat.shape
     steps = ny // ROWS
@@ -187,6 +188,7 @@
         late.append(pltpu.make_async_copy(chk_hbm.at[:, pl.ds(1, inner)], chk.at[:, pl.ds(1, inner)],
                                           load_sem.at[4]))
     seed_load = pltpu.make_async_copy(seed_hbm, seed.at[:, pl.ds(1, width)], load_sem.at[5])
+    loads.append(pltpu.make_async_copy(poro_hbm, poro_ref, load_sem.at[6]))
     for copy in loads + edge_loads + late + [seed_load]:
         copy.start()
 
@@ -202,14 +204,12 @@
     for start, size in ((2, 1), (9, 2), (13, 2)):
         seed_sends.append(remote(seed_hbm.at[pl.ds(start, size), last],
                                  seed.at[pl.ds(start, size), 0], len(seed_sends), right))
-    post_up = remote(post.at[pl.ds(0, 5), width], post.at[pl.ds(0, 5), 0], 6, right)
-    post_down = remote(post.at[pl.ds(5, 5), 1], post.at[pl.ds(5, 5), width + 1], 7, left)
+    post_up = remote(face.at[0], halo.at[0], 6, right)
+    post_down = remote(face.at[1], halo.at[1], 7, left)
     adj_down = remote(adj.at[pl.ds(0, 5), 1], adj.at[pl.ds(0, 5), width + 1], 8, left)
     adj_up = remote(adj.at[pl.ds(5, 5), width], adj.at[pl.ds(5, 5), 0], 9, right)
 
     row = lax.broadcasted_iota(jnp.int32, (ROWS, nz), 0)
-    turn = (step_ref[0] & 63).astype(jnp.float32) * np.float32(2.0 * np.pi / 64.0)
-    force = 0.05 * jnp.sin(jnp.full((ROWS, nz), turn, jnp.float32))
 
     def shifted(ref, slot, layer, i, sy, sz):
         value = ref[slot, layer, pl.ds(pl.multiple_of(i * ROWS, ROWS), ROWS), :]
@@ -222,8 +222,9 @@
             value = pltpu.roll(value, sz % nz, 1)
         return value
 
-    def streamed(ref, x, i, sign, slots):
-        return [shifted(ref, slots[q], x + 1 - sign * VEL[q][0], i, sign * VEL[q][1],
+    def streamed(ref, x, i, sign, slots, without=()):
+        return [jnp.zeros((ROWS, nz), jnp.float32) if VEL[q][0] in without else
+                shifted(ref, slots[q], x + 1 - sign * VEL[q][0], i, sign * VEL[q][1],
                         sign * VEL[q][2]) for q in range(19)]
 
     def over(layers, body):
@@ -235,9 +236,9 @@
             body(first + stride * (t // steps), lax.rem(t, steps))
             return carry
 
-        lax.fori_loop(0, number * steps, step, 0)
-
-    edges = (0, max(last, 1), len(edge))
+        lax.fori_loop(0, number * steps, step, 0, unroll=UNROLL)
+
+    bottom, top = (0, 1, 1), (last, 1, 1)
     middle = (1, 1, inner)
 
     def here(i):
@@ -257,15 +258,37 @@
         for n, value in enumerate((*j, ratio)):
             mom[n, x, at, :] = value
 
-    def back_one(x, i):
+    def fold(x, sign):
+        def body(_, i):
+            moved = {VEL[q][1:]: shifted(post, SLOT[q], x + 1, i, VEL[q][1], VEL[q][2])
+                     for q in (PLUS if sign > 0 else MINUS)}
+            up, down, fore, aft = moved[1, 0], moved[-1, 0], moved[0, 1], moved[0, -1]
+            side = 0 if sign > 0 else 1
+            face[side, 0, here(i), :] = moved[0, 0] + (up + down) + (fore + aft)
+            face[side, 1, here(i), :] = up - down
+            face[side, 2, here(i), :] = fore - aft
+        return body
+
+    def back_one(x, i, folded=()):
         at = here(i)
         porosity = por[x, at, :]
-        density, j = conserved(*to_pairs(streamed(post, x, i, 1, SLOT)))
+        first = streamed(post, x, i, 1, SLOT, [sign for sign, _ in folded])
+        density, j = conserved(*to_pairs(first))
+        for sign, side in folded:
+            total = halo[side, 0, at, :]
+            density = density + total
+            j = (j[0] + sign * total, j[1] + halo[side, 1, at, :], j[2] + halo[side, 2, at, :])
         h = streamed(seed, x, i, -1, SAME)
         a, part = backward(h, j, porosity / density, porosity, wal[x, at, :] == 1)
         for q in range(19):
             adj[SLOT[q], x + 1, at, :] = a[q]
         grad[x, at, :] = part
+
+    def at_bottom(x, i):
+        back_one(x, i, ((1, 0),) if width > 1 else ((1, 0), (-1, 1)))
+
+    def at_top(x, i):
+        back_one(x, i, ((-1, 1),))
 
     def back_zero(x, i):
         at = here(i)
@@ -279,35 +302,55 @@
     pl.semaphore_wait(barrier, 2)
     for copy in seed_sends:
         copy.start()
-    for copy in loads + edge_loads:
+    for copy in loads:
         copy.wait()
-    over(edges, collide)
+    turn = (step_ref[0] & 63).astype(jnp.float32) * np.float32(2.0 * np.pi / 64.0)
+    force = 0.05 * jnp.sin(jnp.full((ROWS, nz), turn, jnp.float32))
+    edge_loads[0].wait()
+    over(bottom, collide)
+    over(bottom, fold(0, -1))
+    post_down.start()
+    if width > 1:
+        edge_loads[1].wait()
+        over(top, collide)
+    over(top, fold(last, 1))
     post_up.start()
-    post_down.start()
     for copy in late:
         copy.wait()
     over(middle, collide)
     seed_load.wait()
     over(middle, back_one)
-    for copy in seed_sends + [post_up, post_down]:
+    from_left, from_right = seed_sends[3:] + [post_up], seed_sends[:3] + [post_down]
+    for copy in from_left if width > 1 else from_left + from_right:
         copy.wait_recv()
-    over(edges, back_one)
+    over(bottom, at_bottom)
+    adj_down.start()
+    if width > 1:
+        for copy in from_right:
+            copy.wait_recv()
+        over(top, at_top)
     adj_up.start()
-    adj_down.start()
     over(middle, back_zero)
     stores = []
+
+    def store(x, size):
+        stores.append(pltpu.make_async_copy(out.at[:, pl.ds(x, size)], out_hbm.at[:, pl.ds(x, size)],
+                                            out_sem.at[len(stores)]))
+        stores[-1].start()
+
     if inner:
-        stores.append(pltpu.make_async_copy(out.at[:, pl.ds(1, inner)], out_hbm.at[:, pl.ds(1, inner)],
-                                            out_sem.at[0]))
-        stores[-1].start()
+        store(1, inner)
     adj_up.wait_recv()
-    adj_down.wait_recv()
-    over(edges, back_zero)
-    for n, x in enumerate(edge):
-        stores.append(pltpu.make_async_copy(out.at[:, x], out_hbm.at[:, x], out_sem.at[1 + n]))
+    if width == 1:
+        adj_down.wait_recv()
+    over(bottom, back_zero)
+    store(0, 1)
+    if width > 1:
+        adj_down.wait_recv()
+        over(top, back_zero)
+        store(last, 1)
     stores.append(pltpu.make_async_copy(grad, grad_hbm, out_sem.at[3]))
-    for copy in stores[-1 - len(edge):]:
-        copy.start()
+    stores[-1].start()
     for copy in seed_sends + [post_up, post_down, adj_up, adj_down]:
         copy.wait_send()
     for copy in stores:
@@ -317,15 +360,16 @@
 def local(checkpoint, adjoint_seed, material, wall_mask, class_porosity, step_index):
     width, ny, nz = material.shape
     f32 = jnp.float32
-    anywhere = pl.BlockSpec(memory_space=pl.ANY)
+    anywhere = pl.BlockSpec(memory_space=pltpu.HBM)
     scalars = pl.BlockSpec(memory_space=pltpu.SMEM)
     return pl.pallas_call(
         functools.partial(kernel, "gx"),
         out_shape=(jax.ShapeDtypeStruct(checkpoint.shape, f32),
                    jax.ShapeDtypeStruct(material.shape, f32)),
-        in_specs=[scalars, scalars] + [anywhere] * 4,
+        in_specs=[anywhere, scalars] + [anywhere] * 4,
         out_specs=(anywhere, anywhere),
         scratch_shapes=[
+            pltpu.SMEM(class_porosity.shape, f32),
             pltpu.VMEM((19, width, ny, nz), f32),
             pltpu.VMEM((width, ny, nz), jnp.int32),
             pltpu.VMEM((width, ny, nz), jnp.int32),
@@ -336,13 +380,15 @@
             pltpu.VMEM((width, ny, nz), f32),
             pltpu.VMEM((19, width, ny, nz), f32),
             pltpu.VMEM((width, ny, nz), f32),
-            pltpu.SemaphoreType.DMA((6,)),
+            pltpu.VMEM((2, 3, ny, nz), f32),
+            pltpu.VMEM((2, 3, ny, nz), f32),
+            pltpu.SemaphoreType.DMA((7,)),
             pltpu.SemaphoreType.DMA((10,)),
             pltpu.SemaphoreType.DMA((10,)),
             pltpu.SemaphoreType.DMA((4,)),
         ],
         compiler_params=pltpu.CompilerParams(
-            collective_id=0, has_side_effects=True, vmem_limit_bytes=44 * 2**20),
+            collective_id=0, has_side_effects=True, vmem_limit_bytes=56 * 2**20),
     )(class_porosity, step_index, checkpoint, adjoint_seed, material, wall_mask)
 
 

time: 32.3 us -> 25.3 us (0.78)
  local copies, waits for them, and re-layouts: 7.97 us -> 4.15 us
  Pallas kernels: 22.8 us -> 19.7 us
    unnamed x12 -> x4, local copies, waits for them, and re-layouts: 7.97 us -> 4.15 us
    pallas_call x1, Pallas kernels: 22.8 us -> 19.7 us  [local(): pl.pallas_call(functools.partial(kernel, 'gx'), out_shape=(jax.ShapeDtype...]
where the time goes in v1:
time: 25.3 us; the launch traced here: 25.1 us
  Pallas kernels  19.7 us (78%)
  local copies, waits for them, and re-layouts  4.15 us (16%)
  between operations  1.29 us (5%)
    pallas_call x1, Pallas kernels, local(): pl.pallas_call(functools.partial(kernel, 'gx'), out_shape=(jax.ShapeDtype...  19.7 us
    unnamed x4, local copies, waits for them, and re-layouts  4.15 us

profile of v1, /device:TPU:0, one launch (start us, length us, event | category | flops | bytes accessed | tf_op | source)
XLA Modules:
  0.0 25.1 jit_solution(13856596299090108047)
XLA Ops:
  1.3 19.7 %shard_map.77 = (f32[19,4,64,128]{3,2,1,0:T(8,128)}, f32[4,64,128]{2,1,0:T(8,128)}) custom-call(f32[8]{0:T(128)} %poro_hbm.1, s32[1]{0:T(128)S(6)} %copy.10.step_ref, f32[19,4,64,128]{3,2,1,0:T(8,128)} %chk_hbm.1, f32[19,4,64,128]{3,2,1,0:T(8,128)} %seed_hbm.1, s32[4,64,128]{2,1,0:T(8,128)} %mat_hbm.1, s32[4,64,128]{2,1,0:T(8,128)} %wall_hbm.1), custom_call_target="tpu_custom_call" | custom-call | tf_op jit(solution)/shard_map/pallas_call | solution.py:365
  21.0 0.0 copy-start
  21.0 3.5 %copy.11 = f32[19,4,64,128]{3,2,1,0:T(8,128)} copy(f32[19,4,64,128]{3,2,1,0:T(8,128)} %get-tuple-element.4) | data formatting | bytes 4980736
  24.5 0.0 copy-done
  24.5 0.7 %copy.12 = f32[4,64,128]{2,1,0:T(8,128)} copy(f32[4,64,128]{2,1,0:T(8,128)S(1)} %copy-done) | data formatting | bytes 262144
Async XLA Ops:
  21.0 3.5 %copy-start = (f32[4,64,128]{2,1,0:T(8,128)S(1)}, f32[4,64,128]{2,1,0:T(8,128)}, u32[]{:S(2)}) copy-start(f32[4,64,128]{2,1,0:T(8,128)} %get-tuple-element.5) | copy-start | bytes 393220

commit v2 on v1

--- a/solution.py
+++ b/solution.py
@@ -163,11 +163,76 @@
     return out, grad
 
 
-def kernel(axis, poro_hbm, step_ref, chk_hbm, seed_hbm, mat_hbm, wall_hbm, out_hbm, grad_hbm,
-           poro_ref, chk, mat, wal, seed, post, adj, mom, por, out, grad, face, halo,
-           load_sem, send_sem, recv_sem, out_sem):
+def here(i):
+    return pl.ds(pl.multiple_of(i * ROWS, ROWS), ROWS)
+
+
+def walkers(ny, nz):
+    steps = ny // ROWS
+
+    def shifted(ref, slot, layer, i, sy, sz):
+        row = lax.broadcasted_iota(jnp.int32, (ROWS, nz), 0)
+        value = ref[slot, layer, pl.ds(pl.multiple_of(i * ROWS, ROWS), ROWS), :]
+        if sy:
+            near = lax.rem(i + (steps - 1 if sy > 0 else 1), steps)
+            other = ref[slot, layer, pl.ds(pl.multiple_of(near * ROWS, ROWS), ROWS), :]
+            value = jnp.where(row == (ROWS - 1 if sy > 0 else 0), other, value)
+            value = pltpu.roll(value, sy % ROWS, 0)
+        if sz:
+            value = pltpu.roll(value, sz % nz, 1)
+        return value
+
+    def streamed(ref, x, i, sign, slots, without=()):
+        return [jnp.zeros((ROWS, nz), jnp.float32) if VEL[q][0] in without else
+                shifted(ref, slots[q], x + 1 - sign * VEL[q][0], i, sign * VEL[q][1],
+                        sign * VEL[q][2]) for q in range(19)]
+
+    def over(layers, body):
+        first, stride, number = layers
+        if number == 0:
+            return
+
+        def step(t, carry):
+            body(first + stride * (t // steps), lax.rem(t, steps))
+            return carry
+
+        lax.fori_loop(0, number * steps, step, 0, unroll=UNROLL)
+
+    return shifted, streamed, over
+
+
+def final_body(streamed, adj, mom, por, wal, out, grad):
+    def back_zero(x, i):
+        at = here(i)
+        h = streamed(adj, x, i, -1, SLOT)
+        j = [mom[n, x, at, :] for n in range(3)]
+        a, part = backward(h, j, mom[3, x, at, :], por[x, at, :], wal[x, at, :] == 1)
+        for q in range(19):
+            out[q, x, at, :] = a[q]
+        grad[x, at, :] = grad[x, at, :] + part
+
+    return back_zero
+
+
+def near_far(axis, width):
+    even = lax.rem(lax.axis_index(axis), 2) == 0
+    return even, jnp.where(even, width - 1, 0), jnp.where(even, 0, width - 1)
+
+
+def finish(done, part, out_hbm, grad_hbm, sem):
+    copies = [pltpu.make_async_copy(done, out_hbm, sem.at[0]),
+              pltpu.make_async_copy(part, grad_hbm, sem.at[1])]
+    for copy in copies:
+        copy.start()
+    for copy in copies:
+        copy.wait()
+
+
+def kernel(axis, poro_hbm, step_ref, chk_hbm, seed_hbm, mat_hbm, wall_hbm,
+           out, grad, poro_ref, chk, mat, wal, mom, por, seed, post, adj, face, halo,
+           load_sem, send_sem, recv_sem):
     width, ny, nz = mat.shape
-    steps = ny // ROWS
+    shifted, streamed, over = walkers(ny, nz)
     count = lax.axis_size(axis)
     me = lax.axis_index(axis)
     right, left = lax.rem(me + 1, count), lax.rem(me + count - 1, count)
@@ -209,40 +274,8 @@
     adj_down = remote(adj.at[pl.ds(0, 5), 1], adj.at[pl.ds(0, 5), width + 1], 8, left)
     adj_up = remote(adj.at[pl.ds(5, 5), width], adj.at[pl.ds(5, 5), 0], 9, right)
 
-    row = lax.broadcasted_iota(jnp.int32, (ROWS, nz), 0)
-
-    def shifted(ref, slot, layer, i, sy, sz):
-        value = ref[slot, layer, pl.ds(pl.multiple_of(i * ROWS, ROWS), ROWS), :]
-        if sy:
-            near = lax.rem(i + (steps - 1 if sy > 0 else 1), steps)
-            other = ref[slot, layer, pl.ds(pl.multiple_of(near * ROWS, ROWS), ROWS), :]
-            value = jnp.where(row == (ROWS - 1 if sy > 0 else 0), other, value)
-            value = pltpu.roll(value, sy % ROWS, 0)
-        if sz:
-            value = pltpu.roll(value, sz % nz, 1)
-        return value
-
-    def streamed(ref, x, i, sign, slots, without=()):
-        return [jnp.zeros((ROWS, nz), jnp.float32) if VEL[q][0] in without else
-                shifted(ref, slots[q], x + 1 - sign * VEL[q][0], i, sign * VEL[q][1],
-                        sign * VEL[q][2]) for q in range(19)]
-
-    def over(layers, body):
-        first, stride, number = layers
-        if number == 0:
-            return
-
-        def step(t, carry):
-            body(first + stride * (t // steps), lax.rem(t, steps))
-            return carry
-
-        lax.fori_loop(0, number * steps, step, 0, unroll=UNROLL)
-
     bottom, top = (0, 1, 1), (last, 1, 1)
     middle = (1, 1, inner)
-
-    def here(i):
-        return pl.ds(pl.multiple_of(i * ROWS, ROWS), ROWS)
 
     def collide(x, i):
         at = here(i)
@@ -290,14 +323,7 @@
     def at_top(x, i):
         back_one(x, i, ((-1, 1),))
 
-    def back_zero(x, i):
-        at = here(i)
-        h = streamed(adj, x, i, -1, SLOT)
-        j = [mom[n, x, at, :] for n in range(3)]
-        a, part = backward(h, j, mom[3, x, at, :], por[x, at, :], wal[x, at, :] == 1)
-        for q in range(19):
-            out[q, x, at, :] = a[q]
-        grad[x, at, :] = grad[x, at, :] + part
+    back_zero = final_body(streamed, adj, mom, por, wal, out, grad)
 
     pl.semaphore_wait(barrier, 2)
     for copy in seed_sends:
@@ -331,30 +357,34 @@
         over(top, at_top)
     adj_up.start()
     over(middle, back_zero)
-    stores = []
-
-    def store(x, size):
-        stores.append(pltpu.make_async_copy(out.at[:, pl.ds(x, size)], out_hbm.at[:, pl.ds(x, size)],
-                                            out_sem.at[len(stores)]))
-        stores[-1].start()
-
-    if inner:
-        store(1, inner)
-    adj_up.wait_recv()
-    if width == 1:
+    if width > 1:
+        even, near, far = near_far(axis, width)
+
+        @pl.when(even)
+        def _():
+            adj_down.wait_recv()
+
+        @pl.when(jnp.logical_not(even))
+        def _():
+            adj_up.wait_recv()
+
+        over((near, 1, 1), back_zero)
+
+        @pl.when(even)
+        def _():
+            adj_up.wait_recv()
+
+        @pl.when(jnp.logical_not(even))
+        def _():
+            adj_down.wait_recv()
+
+        over((far, 1, 1), back_zero)
+    else:
+        adj_up.wait_recv()
         adj_down.wait_recv()
-    over(bottom, back_zero)
-    store(0, 1)
-    if width > 1:
-        adj_down.wait_recv()
-        over(top, back_zero)
-        store(last, 1)
-    stores.append(pltpu.make_async_copy(grad, grad_hbm, out_sem.at[3]))
-    stores[-1].start()
+        over(bottom, back_zero)
     for copy in seed_sends + [post_up, post_down, adj_up, adj_down]:
         copy.wait_send()
-    for copy in stores:
-        copy.wait()
 
 
 def local(checkpoint, adjoint_seed, material, wall_mask, class_porosity, step_index):
@@ -362,34 +392,45 @@
     f32 = jnp.float32
     anywhere = pl.BlockSpec(memory_space=pltpu.HBM)
     scalars = pl.BlockSpec(memory_space=pltpu.SMEM)
-    return pl.pallas_call(
+    vmem = pl.BlockSpec(memory_space=pltpu.VMEM)
+    pinned = lambda x: pltpu.with_memory_space_constraint(x, pltpu.HBM)
+    cells = (width, ny, nz)
+    padded = (19, width + 2, ny, nz)
+    shape = jax.ShapeDtypeStruct
+    kept = pl.pallas_call(
         functools.partial(kernel, "gx"),
-        out_shape=(jax.ShapeDtypeStruct(checkpoint.shape, f32),
-                   jax.ShapeDtypeStruct(material.shape, f32)),
+        out_shape=(shape((19,) + cells, f32), shape(cells, f32)),
         in_specs=[anywhere, scalars] + [anywhere] * 4,
-        out_specs=(anywhere, anywhere),
+        out_specs=(vmem,) * 2,
         scratch_shapes=[
             pltpu.SMEM(class_porosity.shape, f32),
-            pltpu.VMEM((19, width, ny, nz), f32),
-            pltpu.VMEM((width, ny, nz), jnp.int32),
-            pltpu.VMEM((width, ny, nz), jnp.int32),
-            pltpu.VMEM((19, width + 2, ny, nz), f32),
-            pltpu.VMEM((19, width + 2, ny, nz), f32),
-            pltpu.VMEM((19, width + 2, ny, nz), f32),
-            pltpu.VMEM((4, width, ny, nz), f32),
-            pltpu.VMEM((width, ny, nz), f32),
-            pltpu.VMEM((19, width, ny, nz), f32),
-            pltpu.VMEM((width, ny, nz), f32),
+            pltpu.VMEM((19,) + cells, f32),
+            pltpu.VMEM(cells, jnp.int32),
+            pltpu.VMEM(cells, jnp.int32),
+            pltpu.VMEM((4,) + cells, f32),
+            pltpu.VMEM(cells, f32),
+            pltpu.VMEM(padded, f32),
+            pltpu.VMEM(padded, f32),
+            pltpu.VMEM(padded, f32),
             pltpu.VMEM((2, 3, ny, nz), f32),
             pltpu.VMEM((2, 3, ny, nz), f32),
             pltpu.SemaphoreType.DMA((7,)),
             pltpu.SemaphoreType.DMA((10,)),
             pltpu.SemaphoreType.DMA((10,)),
-            pltpu.SemaphoreType.DMA((4,)),
         ],
         compiler_params=pltpu.CompilerParams(
-            collective_id=0, has_side_effects=True, vmem_limit_bytes=56 * 2**20),
-    )(class_porosity, step_index, checkpoint, adjoint_seed, material, wall_mask)
+            collective_id=0, has_side_effects=True, vmem_limit_bytes=28 * 2**20),
+    )(pinned(class_porosity), step_index, pinned(checkpoint), pinned(adjoint_seed),
+      pinned(material), pinned(wall_mask))
+    return pl.pallas_call(
+        finish,
+        out_shape=(shape((19,) + cells, f32), shape(cells, f32)),
+        in_specs=[vmem] * 2,
+        out_specs=(anywhere, anywhere),
+        scratch_shapes=[
+            pltpu.SemaphoreType.DMA((2,)),
+        ],
+    )(*kept)
 
 
 def solution(mesh):

time: 25.3 us -> 25.2 us (level)
  local copies, waits for them, and re-layouts: 4.15 us -> 2.09 us
  Pallas kernels: 19.7 us -> 21.6 us
    unnamed x4, local copies, waits for them, and re-layouts: 4.15 us -> 2.09 us
    pallas_call x1 -> x2, Pallas kernels: 19.7 us -> 21.6 us  [the longest x1 18.4 us: local(): pl.pallas_call(functools.partial(kernel, 'gx'), out_shape=(shape((19,) +...]
where the time goes in v2:
time: 25.2 us; the launch traced here: 25 us
  Pallas kernels  21.6 us (86%)
  local copies, waits for them, and re-layouts  2.09 us (8%)
  between operations  1.3 us (5%)
    pallas_call x1, Pallas kernels, local(): pl.pallas_call(functools.partial(kernel, 'gx'), out_shape=(shape((19,) +...  18.4 us
    pallas_call x1, Pallas kernels, local(): pl.pallas_call(finish, out_shape=(shape((19,) + cells, f32), shape(cells,...  3.19 us
    unnamed x4, local copies, waits for them, and re-layouts  2.09 us

profile of v2, /device:TPU:0, one launch (start us, length us, event | category | flops | bytes accessed | tf_op | source)
XLA Modules:
  0.0 25.0 jit_solution(12732142625205777016)
XLA Ops:
  1.3 18.4 %shard_map.77 = (f32[19,4,64,128]{3,2,1,0:T(8,128)S(1)}, f32[4,64,128]{2,1,0:T(8,128)S(1)}) custom-call(f32[8]{0:T(128)} %poro_hbm.1, s32[1]{0:T(128)S(6)} %copy.8.step_ref, f32[19,4,64,128]{3,2,1,0:T(8,128)} %chk_hbm.1, f32[19,4,64,128]{3,2,1,0:T(8,128)} %seed_hbm.1, s32[4,64,128]{2,1,0:T(8,128)} %mat_hbm.1, s32[4,64,128]{2,1,0:T(8,128)} %wall_hbm.1), custom_call_target="tpu_custom_call" | custom-call | tf_op jit(solution)/shard_map/pallas_call | solution.py:400
  19.7 0.0 copy-start
  19.7 1.4 %copy-done = f32[19,4,64,128]{3,2,1,0:T(8,128)} copy-done((f32[19,4,64,128]{3,2,1,0:T(8,128)}, f32[19,4,64,128]{3,2,1,0:T(8,128)S(1)}, u32[]{:S(2)}) %copy-start) | copy-done | bytes 2490392
  21.2 0.0 copy-start.1
  21.2 0.6 %copy-done.1 = f32[4,64,128]{2,1,0:T(8,128)} copy-done((f32[4,64,128]{2,1,0:T(8,128)}, f32[4,64,128]{2,1,0:T(8,128)S(1)}, u32[]{:S(2)}) %copy-start.1) | copy-done | bytes 131096
  21.8 3.2 %shard_map.78 = (f32[19,4,64,128]{3,2,1,0:T(8,128)}, f32[4,64,128]{2,1,0:T(8,128)}) custom-call(f32[19,4,64,128]{3,2,1,0:T(8,128)} %copy-done, f32[4,64,128]{2,1,0:T(8,128)} %copy-done.1), custom_call_target="tpu_custom_call" | custom-call | tf_op jit(solution)/shard_map/pallas_call | solution.py:425
Async XLA Ops:
  19.7 1.4 %copy-start = (f32[19,4,64,128]{3,2,1,0:T(8,128)}, f32[19,4,64,128]{3,2,1,0:T(8,128)S(1)}, u32[]{:S(2)}) copy-start(f32[19,4,64,128]{3,2,1,0:T(8,128)S(1)} %get-tuple-element.4.done) | copy-start | bytes 7471108
  21.2 0.7 %copy-start.1 = (f32[4,64,128]{2,1,0:T(8,128)}, f32[4,64,128]{2,1,0:T(8,128)S(1)}, u32[]{:S(2)}) copy-start(f32[4,64,128]{2,1,0:T(8,128)S(1)} %get-tuple-element.5.part) | copy-start | bytes 393220

commit v3 on v2

--- a/solution.py
+++ b/solution.py
@@ -220,8 +220,10 @@
 
 
 def finish(done, part, out_hbm, grad_hbm, sem):
-    copies = [pltpu.make_async_copy(done, out_hbm, sem.at[0]),
-              pltpu.make_async_copy(part, grad_hbm, sem.at[1])]
+    copies = [pltpu.make_async_copy(done.at[pl.ds(q, min(5, 19 - q))],
+                                    out_hbm.at[pl.ds(q, min(5, 19 - q))], sem.at[q // 5])
+              for q in range(0, 19, 5)]
+    copies.append(pltpu.make_async_copy(part, grad_hbm, sem.at[4]))
     for copy in copies:
         copy.start()
     for copy in copies:
@@ -428,8 +430,9 @@
         in_specs=[vmem] * 2,
         out_specs=(anywhere, anywhere),
         scratch_shapes=[
-            pltpu.SemaphoreType.DMA((2,)),
+            pltpu.SemaphoreType.DMA((5,)),
         ],
+        compiler_params=pltpu.CompilerParams(vmem_limit_bytes=8 * 2**20),
     )(*kept)
 
 

time: 25.2 us -> 21.4 us (0.85)
  local copies, waits for them, and re-layouts: 2.09 us -> 0 us
  Pallas kernels: 21.6 us -> 19.9 us
    unnamed x4 -> x0, local copies, waits for them, and re-layouts: 2.09 us -> none
    pallas_call x1, Pallas kernels: 3.19 us -> 1.52 us  [local(): pl.pallas_call(finish, out_shape=(shape((19,) + cells, f32), shape(cells,...]
where the time goes in v3:
time: 21.4 us; the launch traced here: 21.2 us
  Pallas kernels  19.9 us (93%)
  between operations  1.29 us (6%)
    pallas_call x1, Pallas kernels, local(): pl.pallas_call(functools.partial(kernel, 'gx'), out_shape=(shape((19,) +...  18.4 us
    pallas_call x1, Pallas kernels, local(): pl.pallas_call(finish, out_shape=(shape((19,) + cells, f32), shape(cells,...  1.52 us

profile of v3, /device:TPU:0, one launch (start us, length us, event | category | flops | bytes accessed | tf_op | source)
XLA Modules:
  0.0 21.2 jit_solution(11018079877345262564)
XLA Ops:
  1.3 18.4 %shard_map.77 = (f32[19,4,64,128]{3,2,1,0:T(8,128)S(1)}, f32[4,64,128]{2,1,0:T(8,128)S(1)}) custom-call(f32[8]{0:T(128)} %poro_hbm.1, s32[1]{0:T(128)S(6)} %copy.8.step_ref, f32[19,4,64,128]{3,2,1,0:T(8,128)} %chk_hbm.1, f32[19,4,64,128]{3,2,1,0:T(8,128)} %seed_hbm.1, s32[4,64,128]{2,1,0:T(8,128)} %mat_hbm.1, s32[4,64,128]{2,1,0:T(8,128)} %wall_hbm.1), custom_call_target="tpu_custom_call" | custom-call | tf_op jit(solution)/shard_map/pallas_call | solution.py:402
  19.7 1.5 %shard_map.78 = (f32[19,4,64,128]{3,2,1,0:T(8,128)}, f32[4,64,128]{2,1,0:T(8,128)}) custom-call(f32[19,4,64,128]{3,2,1,0:T(8,128)S(1)} %get-tuple-element.4.done, f32[4,64,128]{2,1,0:T(8,128)S(1)} %get-tuple-element.5.part), custom_call_target="tpu_custom_call" | custom-call | tf_op jit(solution)/shard_map/pallas_call | solution.py:427

commit v4 on v3

--- a/solution.py
+++ b/solution.py
@@ -327,22 +327,61 @@
 
     back_zero = final_body(streamed, adj, mom, por, wal, out, grad)
 
-    pl.semaphore_wait(barrier, 2)
-    for copy in seed_sends:
-        copy.start()
-    for copy in loads:
-        copy.wait()
     turn = (step_ref[0] & 63).astype(jnp.float32) * np.float32(2.0 * np.pi / 64.0)
     force = 0.05 * jnp.sin(jnp.full((ROWS, nz), turn, jnp.float32))
-    edge_loads[0].wait()
-    over(bottom, collide)
-    over(bottom, fold(0, -1))
-    post_down.start()
+    even, near, far = near_far(axis, width)
+
+    def by_side(first, second):
+        @pl.when(even)
+        def _():
+            first()
+
+        second()
+
+        @pl.when(jnp.logical_not(even))
+        def _():
+            first()
+
+    def send_seeds(group):
+        for copy in group:
+            copy.start()
+
+    def send_bottom():
+        over(bottom, fold(0, -1))
+        post_down.start()
+
+    def send_top():
+        over(top, fold(last, 1))
+        post_up.start()
+
+    pl.semaphore_wait(barrier, 2)
+    by_side(lambda: send_seeds(seed_sends[:3]), lambda: send_seeds(seed_sends[3:]))
+    for copy in loads + edge_loads:
+        copy.wait()
     if width > 1:
-        edge_loads[1].wait()
-        over(top, collide)
-    over(top, fold(last, 1))
-    post_up.start()
+        over((far, 1, 1), collide)
+
+        @pl.when(even)
+        def _():
+            send_bottom()
+
+        @pl.when(jnp.logical_not(even))
+        def _():
+            send_top()
+
+        over((near, 1, 1), collide)
+
+        @pl.when(even)
+        def _():
+            send_top()
+
+        @pl.when(jnp.logical_not(even))
+        def _():
+            send_bottom()
+    else:
+        over(bottom, collide)
+        send_bottom()
+        send_top()
     for copy in late:
         copy.wait()
     over(middle, collide)
@@ -360,8 +399,6 @@
     adj_up.start()
     over(middle, back_zero)
     if width > 1:
-        even, near, far = near_far(axis, width)
-
         @pl.when(even)
         def _():
             adj_down.wait_recv()

time: 21.4 us -> 21.4 us (level)
  no operation moved by 1% of the time
where the time goes in v4:
time: 21.4 us; the launch traced here: 21.2 us
  Pallas kernels  19.9 us (93%)
  between operations  1.29 us (6%)
    pallas_call x1, Pallas kernels, local(): pl.pallas_call(functools.partial(kernel, 'gx'), out_shape=(shape((19,) +...  18.4 us
    pallas_call x1, Pallas kernels, local(): pl.pallas_call(finish, out_shape=(shape((19,) + cells, f32), shape(cells,...  1.52 us

profile of v4, /device:TPU:0, one launch (start us, length us, event | category | flops | bytes accessed | tf_op | source)
XLA Modules:
  0.0 21.2 jit_solution(1177769956333107862)
XLA Ops:
  1.3 18.4 %shard_map.77 = (f32[19,4,64,128]{3,2,1,0:T(8,128)S(1)}, f32[4,64,128]{2,1,0:T(8,128)S(1)}) custom-call(f32[8]{0:T(128)} %poro_hbm.1, s32[1]{0:T(128)S(6)} %copy.8.step_ref, f32[19,4,64,128]{3,2,1,0:T(8,128)} %chk_hbm.1, f32[19,4,64,128]{3,2,1,0:T(8,128)} %seed_hbm.1, s32[4,64,128]{2,1,0:T(8,128)} %mat_hbm.1, s32[4,64,128]{2,1,0:T(8,128)} %wall_hbm.1), custom_call_target="tpu_custom_call" | custom-call | tf_op jit(solution)/shard_map/pallas_call | solution.py:439
  19.7 1.5 %shard_map.78 = (f32[19,4,64,128]{3,2,1,0:T(8,128)}, f32[4,64,128]{2,1,0:T(8,128)}) custom-call(f32[19,4,64,128]{3,2,1,0:T(8,128)S(1)} %get-tuple-element.4.done, f32[4,64,128]{2,1,0:T(8,128)S(1)} %get-tuple-element.5.part), custom_call_target="tpu_custom_call" | custom-call | tf_op jit(solution)/shard_map/pallas_call | solution.py:464

commit v5 on v4

--- a/solution.py
+++ b/solution.py
@@ -273,8 +273,16 @@
                                  seed.at[pl.ds(start, size), 0], len(seed_sends), right))
     post_up = remote(face.at[0], halo.at[0], 6, right)
     post_down = remote(face.at[1], halo.at[1], 7, left)
-    adj_down = remote(adj.at[pl.ds(0, 5), 1], adj.at[pl.ds(0, 5), width + 1], 8, left)
-    adj_up = remote(adj.at[pl.ds(5, 5), width], adj.at[pl.ds(5, 5), 0], 9, right)
+    adj_down = [remote(adj.at[q, 1], adj.at[q, width + 1], 8 + q, left) for q in range(5)]
+    adj_up = [remote(adj.at[q, width], adj.at[q, 0], 8 + q, right) for q in range(5, 10)]
+
+    def start(copies):
+        for copy in copies:
+            copy.start()
+
+    def arrive(copies):
+        for copy in copies:
+            copy.wait_recv()
 
     bottom, top = (0, 1, 1), (last, 1, 1)
     middle = (1, 1, inner)
@@ -391,38 +399,38 @@
     for copy in from_left if width > 1 else from_left + from_right:
         copy.wait_recv()
     over(bottom, at_bottom)
-    adj_down.start()
+    start(adj_down)
     if width > 1:
         for copy in from_right:
             copy.wait_recv()
         over(top, at_top)
-    adj_up.start()
+    start(adj_up)
     over(middle, back_zero)
     if width > 1:
         @pl.when(even)
         def _():
-            adj_down.wait_recv()
+            arrive(adj_down)
 
         @pl.when(jnp.logical_not(even))
         def _():
-            adj_up.wait_recv()
+            arrive(adj_up)
 
         over((near, 1, 1), back_zero)
 
         @pl.when(even)
         def _():
-            adj_up.wait_recv()
+            arrive(adj_up)
 
         @pl.when(jnp.logical_not(even))
         def _():
-            adj_down.wait_recv()
+            arrive(adj_down)
 
         over((far, 1, 1), back_zero)
     else:
-        adj_up.wait_recv()
-        adj_down.wait_recv()
+        arrive(adj_up)
+        arrive(adj_down)
         over(bottom, back_zero)
-    for copy in seed_sends + [post_up, post_down, adj_up, adj_down]:
+    for copy in seed_sends + [post_up, post_down] + adj_up + adj_down:
         copy.wait_send()
 
 
@@ -454,8 +462,8 @@
             pltpu.VMEM((2, 3, ny, nz), f32),
             pltpu.VMEM((2, 3, ny, nz), f32),
             pltpu.SemaphoreType.DMA((7,)),
-            pltpu.SemaphoreType.DMA((10,)),
-            pltpu.SemaphoreType.DMA((10,)),
+            pltpu.SemaphoreType.DMA((18,)),
+            pltpu.SemaphoreType.DMA((18,)),
         ],
         compiler_params=pltpu.CompilerParams(
             collective_id=0, has_side_effects=True, vmem_limit_bytes=28 * 2**20),

time: 21.4 us -> 21.5 us (level)
  no operation moved by 1% of the time
where the time goes in v5:
time: 21.5 us; the launch traced here: 21.4 us
  Pallas kernels  20.1 us (93%)
  between operations  1.29 us (6%)
    pallas_call x1, Pallas kernels, local(): pl.pallas_call(functools.partial(kernel, 'gx'), out_shape=(shape((19,) +...  18.6 us
    pallas_call x1, Pallas kernels, local(): pl.pallas_call(finish, out_shape=(shape((19,) + cells, f32), shape(cells,...  1.52 us

profile of v5, /device:TPU:0, one launch (start us, length us, event | category | flops | bytes accessed | tf_op | source)
XLA Modules:
  0.0 21.4 jit_solution(6586243025928272272)
XLA Ops:
  1.3 18.6 %shard_map.77 = (f32[19,4,64,128]{3,2,1,0:T(8,128)S(1)}, f32[4,64,128]{2,1,0:T(8,128)S(1)}) custom-call(f32[8]{0:T(128)} %poro_hbm.1, s32[1]{0:T(128)S(6)} %copy.8.step_ref, f32[19,4,64,128]{3,2,1,0:T(8,128)} %chk_hbm.1, f32[19,4,64,128]{3,2,1,0:T(8,128)} %seed_hbm.1, s32[4,64,128]{2,1,0:T(8,128)} %mat_hbm.1, s32[4,64,128]{2,1,0:T(8,128)} %wall_hbm.1), custom_call_target="tpu_custom_call" | custom-call | tf_op jit(solution)/shard_map/pallas_call | solution.py:447
  19.9 1.5 %shard_map.78 = (f32[19,4,64,128]{3,2,1,0:T(8,128)}, f32[4,64,128]{2,1,0:T(8,128)}) custom-call(f32[19,4,64,128]{3,2,1,0:T(8,128)S(1)} %get-tuple-element.4.done, f32[4,64,128]{2,1,0:T(8,128)S(1)} %get-tuple-element.5.part), custom_call_target="tpu_custom_call" | custom-call | tf_op jit(solution)/shard_map/pallas_call | solution.py:472
